TPU v7x, 32 devices: a whole 2x2x4 slice. The times are simulated.
32 devices in a mesh: chan: 16 (over z, x, core), rows: 2 (over y).
Axes of the slice: x: 2, y: 2, z: 4, core: 2. Of those that a mesh axis runs over, the one named last changes fastest.
Arguments:
- inputs: bfloat16 [1, 2, 256, 2048], P(None, 'rows', None, 'chan'), may hold values from -6 to 6
- weights: bfloat16 [3, 3, 2048, 2048], P(None, None, 'chan'), may hold values from -0.0625 to 0.0625
- cotangent: bfloat16 [1, 2, 256, 2048], P(None, 'rows', None, 'chan'), may hold values from -6 to 6
Outputs:
- outputs: bfloat16 [1, 2, 256, 2048], P(None, 'rows', None, 'chan')
- input_grad: bfloat16 [1, 2, 256, 2048], P(None, 'rows', None, 'chan')
- weight_grad: float32 [3, 3, 2048, 2048], P(None, None, 'chan', 'rows')
All inputs are finite; a program needn't handle non-finite values.
Results may differ from a plain program's by a relative error of at most 0.001.
Values may be sent and summed in bfloat16 or wider, within the bound.
A program may use at most 128 MiB of HBM per device.

v0:
```python
import jax
import jax.numpy as jnp
from jax import lax
from jax.sharding import PartitionSpec as P


def with_halo(array, sides, width):
    for axis, dim in sides:
        devices, length = (lax.axis_size(axis), array.shape[dim])
        up = [(i, (i + 1) % devices) for i in range(devices - 1)]
        down = [(j, i) for i, j in up]
        last = lax.slice_in_dim(array, length - width, length, axis=dim)
        initial = lax.slice_in_dim(array, 0, width, axis=dim)
        before = lax.ppermute(last, axis, up)
        after = lax.ppermute(initial, axis, down)
        array = jnp.concatenate([before, array, after], axis=dim)
    return array


def unfold(padded, height, breadth):
    taps = [
        padded[:, row_off : row_off + height, col_off : col_off + breadth, :]
        for row_off in range(3)
        for col_off in range(3)
    ]
    stacked = jnp.concatenate(taps, axis=3)
    return stacked.reshape(-1, stacked.shape[3])


def pad_columns(rimmed):
    return jnp.pad(rimmed, ((0, 0), (0, 0), (1, 1), (0, 0)))


def on_device(inputs, weights, cotangent):
    batches = inputs.shape[0]
    height = inputs.shape[1]
    breadth = inputs.shape[2]
    local_ch = inputs.shape[3]
    channels = weights.shape[3]
    pixels = batches * height * breadth
    contract_first = (((0,), (1,)), ((), ()))
    rimmed = with_halo(inputs, (("rows", 1),), 1)
    columns = unfold(pad_columns(rimmed), height, breadth)
    matrix = weights.reshape(9 * local_ch, channels)
    block = matrix
    conv_out = lax.psum_scatter(
        lax.dot_general(block, columns, contract_first, preferred_element_type=jnp.float32),
        "chan",
        scatter_dimension=0,
        tiled=True,
    )
    outputs = conv_out.T.reshape(batches, height, breadth, local_ch).astype(jnp.bfloat16)
    grad_rimmed = with_halo(cotangent, (("rows", 1),), 1)
    flipped = jnp.transpose(weights[::-1, ::-1], (2, 0, 1, 3))
    piece = lax.all_gather(grad_rimmed, "chan", axis=3, tiled=True)
    count = piece.shape[3]
    grad_cols = unfold(pad_columns(piece), height, breadth)
    block = flipped.reshape(local_ch, 9 * count)
    data_sum = lax.dot_general(
        block, grad_cols, (((1,), (1,)), ((), ())), preferred_element_type=jnp.float32
    )
    inner = piece[:, 1 : height + 1].reshape(pixels, count)
    update = lax.dot_general(
        columns, inner, (((0,), (0,)), ((), ())), preferred_element_type=jnp.float32
    )
    filter_sum = update
    data_sum, filter_sum = (data_sum, filter_sum)
    input_grad = data_sum.T.reshape(batches, height, breadth, local_ch).astype(jnp.bfloat16)
    total_pixels = pixels * lax.axis_size("rows")
    scaled = (filter_sum / jnp.sqrt(jnp.float32(total_pixels))).reshape(3, 3, local_ch, channels)
    weight_grad = lax.psum_scatter(scaled, "rows", scatter_dimension=3, tiled=True)
    return (outputs, input_grad, weight_grad)


def solution(mesh):
    in_specs = (
        P(None, "rows", None, "chan"),
        P(None, None, "chan", None),
        P(None, "rows", None, "chan"),
    )
    out_specs = (
        P(None, "rows", None, "chan"),
        P(None, "rows", None, "chan"),
        P(None, None, "chan", "rows"),
    )
    return jax.shard_map(
        on_device, mesh=mesh, in_specs=in_specs, out_specs=out_specs, check_vma=False
    )
```

profile of v0, /device:TPU:0, one launch (start us, length us, event | category | flops | bytes accessed | tf_op | source)
XLA Modules:
  0.0 250.3 jit_solution(17633905704568887612)
XLA Ops:
  7.2 0.0 all-gather.2.cloned.1.call-start
  7.2 4.9 %collective-permute-start.2 = (bf16[1,1,256,128]{3,2,1,0:T(8,128)(2,1)}, bf16[1,1,256,128]{3,2,1,0:T(8,128)(2,1)S(1)}, u32[]{:S(2)}, u32[]{:S(2)}) collective-permute-start(bf16[1,1,256,128]{3,2,1,0:T(8,128)(2,1)} %param.5), channel_id=1, source_target_pairs={{0,1},{2,3},{4,5},{6,7},{8,9},{10,11},{12,13},{14,15},{16,17},{18,... | collective-permute-start | bytes 196616 | tf_op jit(solution)/shard_map/ppermute | solution.py:14
  12.1 1.3 collective-permute-start.3
  13.4 0.9 collective-permute-done.2
  14.3 4.2 %collective-permute-done.3 = bf16[1,1,256,128]{3,2,1,0:T(8,128)(2,1)S(1)} collective-permute-done((bf16[1,1,256,128]{3,2,1,0:T(8,128)(2,1)}, bf16[1,1,256,128]{3,2,1,0:T(8,128)(2,1)S(1)}, u32[]{:S(2)}, u32[]{:S(2)}) %collective-permute-start.3) | collective-permute-done | bytes 65568 | tf_op jit(solution)/shard_map/ppermute | solution.py:15
  18.5 1.5 pad_maximum_fusion
  20.0 0.0 all-gather.2.cloned.1.call-update
  20.0 0.0 reduce-scatter.3.cloned.1.call-start
  20.1 1.7 collective-permute-start
  21.8 1.3 collective-permute-start.1
  23.1 0.9 collective-permute-done
  24.0 4.2 %collective-permute-done.1 = bf16[1,1,256,128]{3,2,1,0:T(8,128)(2,1)S(1)} collective-permute-done((bf16[1,1,256,128]{3,2,1,0:T(8,128)(2,1)}, bf16[1,1,256,128]{3,2,1,0:T(8,128)(2,1)S(1)}, u32[]{:S(2)}, u32[]{:S(2)}) %collective-permute-start.1) | collective-permute-done | bytes 65568 | tf_op jit(solution)/shard_map/ppermute | solution.py:15
  28.1 0.9 fusion.23
  29.1 0.9 constant_dynamic-update-slice_fusion.1
  30.1 5.2 %convolution_bitcast_fusion = f32[2048,256]{0,1:T(8,128)} fusion(bf16[1152,2048]{1,0:T(8,128)(2,1)} %bitcast.34, bf16[1,1,256,1152]{3,2,1,0:T(8,128)(2,1)S(1)} %slice_dynamic-update-slice_fusion.3), kind=kOutput, calls=%fused_computation.3 | convolution fusion | flops 1207959552 | bytes 7405568 | tf_op jit(solution)/shard_map/dot_general | solution.py:47
  35.4 0.0 reduce-scatter.3.cloned.1.call-update
  35.4 0.0 reduce-scatter.5.cloned.1.call-start
  35.4 32.2 %all-gather.2.cloned.1.call-done = bf16[1,3,256,2048]{3,2,1,0:T(8,128)(2,1)} async-done(((bf16[1,3,256,128]{3,2,1,0:T(8,128)(2,1)}), bf16[1,3,256,2048]{3,2,1,0:T(8,128)(2,1)}) %all-gather.2.cloned.1.call-update) | async-done | bytes 3145744 | tf_op jit(solution)/shard_map/all_gather | solution.py:55
  67.7 6.3 %convolution_multiply_fusion = f32[1152,2048]{1,0:T(8,128)} fusion(bf16[1,3,256,2048]{3,2,1,0:T(8,128)(2,1)} %all-gather.2.cloned.1.call-done, bf16[1,1,256,1152]{3,2,1,0:T(8,128)(2,1)S(1)} %slice_dynamic-update-slice_fusion.3), kind=kOutput, calls=%fused_computation | convolution fusion | flops 1210318848 | bytes 11075584 | tf_op jit(solution)/shard_map/dot_general | solution.py:63
  74.0 0.0 reduce-scatter.5.cloned.1.call-update
  74.0 0.0 copy-start
  74.0 6.9 %copy.6 = bf16[3,3,128,2048]{2,3,1,0:T(8,128)(2,1)} copy(bf16[3,3,128,2048]{3,2,1,0:T(8,128)(2,1)} %param.4) | data formatting | bytes 9437184 | tf_op args[1]
  80.9 5.0 %rev.3 = bf16[3,3,128,2048]{2,3,1,0:T(8,128)(2,1)} reverse(bf16[3,3,128,2048]{2,3,1,0:T(8,128)(2,1)} %copy.6), dimensions={0,1} | reverse | bytes 9437184 | tf_op jit(solution)/shard_map/rev | solution.py:54
  85.9 45.3 %reduce-scatter.3.cloned.1.call-done = f32[128,256]{0,1:T(8,128)} async-done(((f32[2048,256]{0,1:T(8,128)}), f32[128,256]{0,1:T(8,128)}) %reduce-scatter.3.cloned.1.call-update) | async-done | bytes 131088 | tf_op jit(solution)/shard_map/reduce_scatter | solution.py:46
  131.2 1.5 convert_bitcast_fusion
  132.7 0.0 copy-done
  132.7 0.3 fusion.8
  133.0 0.1 slice_dynamic-update-slice_fusion.1
  133.1 0.2 fusion.9
  133.3 0.3 fusion.10
  133.6 0.0 slice-start
  133.6 0.1 slice_dynamic-update-slice_fusion.2
  133.7 0.2 fusion.11
  133.9 0.0 slice-start.1
  134.0 0.3 fusion.12
  134.2 0.1 slice_dynamic-update-slice_fusion
  134.3 0.2 fusion.13
  134.6 1.2 slice-done
  135.8 0.2 slice-done.1
  136.0 3.2 %fusion.5 = bf16[1,1,256,128]{3,2,1,0:T(8,128)(2,1)} fusion(bf16[128,18432]{0,1:T(8,128)(2,1)S(1)} %bitcast.33, bf16[1,1,256,18432]{3,2,1,0:T(8,128)(2,1)S(1)} %fusion.13), kind=kOutput, calls=%fused_computation.11 | convolution fusion | flops 1207992320 | bytes 14221312 | tf_op jit(solution)/shard_map/dot_general | solution.py:59
  139.2 104.6 %reduce-scatter.5.cloned.1.call-done = f32[3,3,128,1024]{3,2,1,0:T(8,128)} async-done(((f32[3,3,128,2048]{3,2,1,0:T(8,128)}), f32[3,3,128,1024]{3,2,1,0:T(8,128)}) %reduce-scatter.5.cloned.1.call-update) | async-done | bytes 4718608 | tf_op jit(solution)/shard_map/reduce_scatter | solution.py:71
  (9 shorter events, 0.2 us)
Async XLA Ops:
  7.2 60.5 %all-gather.2.cloned.1.call-start = ((), (), s32[]{:S(2)}) async-start(), calls=%async_computation.3 | async-start | bytes 3342336 | tf_op jit(solution)/shard_map/all_gather | solution.py:55
  7.2 7.1 %collective-permute-start.2 = (bf16[1,1,256,128]{3,2,1,0:T(8,128)(2,1)}, bf16[1,1,256,128]{3,2,1,0:T(8,128)(2,1)S(1)}, u32[]{:S(2)}, u32[]{:S(2)}) collective-permute-start(bf16[1,1,256,128]{3,2,1,0:T(8,128)(2,1)} %param.5), channel_id=1, source_target_pairs={{0,1},{2,3},{4,5},{6,7},{8,9},{10,11},{12,13},{14,15},{16,17},{18,... | collective-permute-start | bytes 196616 | tf_op jit(solution)/shard_map/ppermute | solution.py:14
  12.1 6.4 %collective-permute-start.3 = (bf16[1,1,256,128]{3,2,1,0:T(8,128)(2,1)}, bf16[1,1,256,128]{3,2,1,0:T(8,128)(2,1)S(1)}, u32[]{:S(2)}, u32[]{:S(2)}) collective-permute-start(bf16[1,1,256,128]{3,2,1,0:T(8,128)(2,1)} %param.5), channel_id=1, source_target_pairs={{1,0},{3,2},{5,4},{7,6},{9,8},{11,10},{13,12},{15,14},{17,16},{19,... | collective-permute-start | bytes 196616 | tf_op jit(solution)/shard_map/ppermute | solution.py:15
  20.0 111.2 %reduce-scatter.3.cloned.1.call-start = ((), (), s32[]{:S(2)}) async-start(), calls=%async_computation.2 | async-start | bytes 2228224 | tf_op jit(solution)/shard_map/reduce_scatter | solution.py:46
  20.1 3.9 %collective-permute-start = (bf16[1,1,256,128]{3,2,1,0:T(8,128)(2,1)}, bf16[1,1,256,128]{3,2,1,0:T(8,128)(2,1)S(1)}, u32[]{:S(2)}, u32[]{:S(2)}) collective-permute-start(bf16[1,1,256,128]{3,2,1,0:T(8,128)(2,1)} %param.3), channel_id=1, source_target_pairs={{0,1},{2,3},{4,5},{6,7},{8,9},{10,11},{12,13},{14,15},{16,17},{18,... | collective-permute-start | bytes 196616 | tf_op jit(solution)/shard_map/ppermute | solution.py:14
  21.8 6.4 %collective-permute-start.1 = (bf16[1,1,256,128]{3,2,1,0:T(8,128)(2,1)}, bf16[1,1,256,128]{3,2,1,0:T(8,128)(2,1)S(1)}, u32[]{:S(2)}, u32[]{:S(2)}) collective-permute-start(bf16[1,1,256,128]{3,2,1,0:T(8,128)(2,1)} %param.3), channel_id=1, source_target_pairs={{1,0},{3,2},{5,4},{7,6},{9,8},{11,10},{13,12},{15,14},{17,16},{19,... | collective-permute-start | bytes 196616 | tf_op jit(solution)/shard_map/ppermute | solution.py:15
  35.4 208.4 %reduce-scatter.5.cloned.1.call-start = ((), (), s32[]{:S(2)}) async-start(), calls=%async_computation.4 | async-start | bytes 14155776 | tf_op jit(solution)/shard_map/reduce_scatter | solution.py:71
  74.0 58.7 %copy-start = (bf16[1,3,256,2048]{3,2,1,0:T(8,128)(2,1)S(1)}, bf16[1,3,256,2048]{3,2,1,0:T(8,128)(2,1)}, u32[]{:S(2)}) copy-start(bf16[1,3,256,2048]{3,2,1,0:T(8,128)(2,1)} %all-gather.2.cloned.1.call-done) | copy-start | bytes 9437188
  133.6 2.2 slice-start
  133.9 2.0 slice-start.1
Sparse Core Ops, SparseCore 0:
  20.1 47.4 all-gather.1
  71.4 59.7 reduce-scatter.2
  134.2 109.5 reduce-scatter.4
where the time goes:
time: 251 us; the launch traced here: 250 us
  waiting for transfers between devices  192 us (76%)
  local copies, waits for them, and re-layouts  16.1 us (6%)
  matrix products  14.8 us (6%)
  between operations  13.9 us (6%)
  starting transfers between devices  9.26 us (4%)
  other arithmetic  3.98 us (2%)
    reduce_scatter x1, waiting for transfers between devices, on_device(): lax.psum_scatter(scaled, 'rows', scatter_dimension=3, tiled=True)  105 us
    reduce_scatter x1, waiting for transfers between devices, on_device(): lax.psum_scatter(lax.dot_general(block, columns, contract_first, preferre...  45.3 us
    all_gather x1, waiting for transfers between devices, on_device(): piece = lax.all_gather(grad_rimmed, 'chan', axis=3, tiled=True)  32.2 us
    unnamed x23, local copies, waits for them, and re-layouts  10.8 us
    ppermute x2, waiting for transfers between devices, with_halo(): after = lax.ppermute(initial, axis, down)  8.34 us
    ppermute x2, starting transfers between devices, with_halo(): before = lax.ppermute(last, axis, up)  6.55 us
    dot_general x1, matrix products, on_device(): lax.dot_general(columns, inner, (((0,), (0,)), ((), ())), preferred_eleme...  6.29 us
    dot_general x1, matrix products, on_device(): lax.dot_general(block, columns, contract_first, preferred_element_type=jn...  5.22 us
  transfers between devices with their start and end apart: 7, of which 7 were waited for; matrix products, arithmetic and copies ran while one was open for 13% of the time, Pallas kernels for 0%

commit v1 on v0

--- a/solution.py
+++ b/solution.py
@@ -52,7 +52,23 @@
     outputs = conv_out.T.reshape(batches, height, breadth, local_ch).astype(jnp.bfloat16)
     grad_rimmed = with_halo(cotangent, (("rows", 1),), 1)
     flipped = jnp.transpose(weights[::-1, ::-1], (2, 0, 1, 3))
-    piece = lax.all_gather(grad_rimmed, "chan", axis=3, tiled=True)
+    ways, here, turn = (lax.axis_size("chan"), lax.axis_index("chan"), grad_rimmed.shape[3])
+    dims = [n * ways if d == 3 else n for d, n in enumerate(grad_rimmed.shape)]
+    full = lax.dynamic_update_slice_in_dim(
+        jnp.zeros(dims, grad_rimmed.dtype), grad_rimmed, here * turn, axis=3
+    )
+    going_up = going_down = grad_rimmed
+    for far in range(1, ways // 2 + 1):
+        going_up = lax.ppermute(going_up, "chan", [(d, (d + 1) % ways) for d in range(ways)])
+        full = lax.dynamic_update_slice_in_dim(full, going_up, (here - far) % ways * turn, axis=3)
+        if 2 * far < ways:
+            going_down = lax.ppermute(
+                going_down, "chan", [(d, (d - 1) % ways) for d in range(ways)]
+            )
+            full = lax.dynamic_update_slice_in_dim(
+                full, going_down, (here + far) % ways * turn, axis=3
+            )
+    piece = full
     count = piece.shape[3]
     grad_cols = unfold(pad_columns(piece), height, breadth)
     block = flipped.reshape(local_ch, 9 * count)

time: 251 us -> 221 us (0.88)
  waiting for transfers between devices: 192 us -> 130 us
  starting transfers between devices: 9.26 us -> 41 us
  local copies, waits for them, and re-layouts: 16.1 us -> 19 us
    reduce_scatter x1, waiting for transfers between devices: 45.3 us -> 0.01 us  [on_device(): lax.psum_scatter(lax.dot_general(block, columns, contract_first, preferre...]
    ppermute x0 -> x15, waiting for transfers between devices: none -> 33.2 us  [the longest x8 30.8 us: on_device(): lax.ppermute(going_up, 'chan', [(d, (d + 1) % ways) for d in range(ways)])]
    all_gather x1 -> x0, waiting for transfers between devices: 32.2 us -> none  [on_device(): piece = lax.all_gather(grad_rimmed, 'chan', axis=3, tiled=True)]
    ppermute x0 -> x15, starting transfers between devices: none -> 31.8 us  [the longest x7 31.7 us: on_device(): lax.ppermute(going_down, 'chan', [(d, (d - 1) % ways) for d in range(ways)])]
    reduce_scatter x1, waiting for transfers between devices: 105 us -> 87.3 us  [on_device(): lax.psum_scatter(scaled, 'rows', scatter_dimension=3, tiled=True)]
    unnamed x23 -> x29, local copies, waits for them, and re-layouts: 10.8 us -> 11.6 us
  transfers between devices with their start and end apart: 7 -> 21, of which waited for: 7 -> 15; matrix products, arithmetic and copies ran while one was open for 13% -> 12% of each run, Pallas kernels for 0% -> 0%
where the time goes in v1:
time: 221 us
  waiting for transfers between devices  130 us (59%)
  starting transfers between devices  41 us (19%)
  local copies, waits for them, and re-layouts  19 us (9%)
  between operations  14.4 us (7%)
  matrix products  13.6 us (6%)
  other arithmetic  2.47 us (1%)
    reduce_scatter x1, waiting for transfers between devices, on_device(): lax.psum_scatter(scaled, 'rows', scatter_dimension=3, tiled=True)  87.3 us
    ppermute x7, starting transfers between devices, on_device(): lax.ppermute(going_down, 'chan', [(d, (d - 1) % ways) for d in range(ways)])  31.7 us
    ppermute x8, waiting for transfers between devices, on_device(): lax.ppermute(going_up, 'chan', [(d, (d + 1) % ways) for d in range(ways)])  30.8 us
    unnamed x29, local copies, waits for them, and re-layouts  11.6 us
    ppermute x2, waiting for transfers between devices, with_halo(): after = lax.ppermute(initial, axis, down)  8.43 us
    ppermute x2, starting transfers between devices, with_halo(): before = lax.ppermute(last, axis, up)  6.56 us
    dot_general x1, matrix products, on_device(): lax.dot_general(block, columns, contract_first, preferred_element_type=jn...  5.25 us
    dot_general x1, matrix products, on_device(): lax.dot_general(columns, inner, (((0,), (0,)), ((), ())), preferred_eleme...  5.1 us
  transfers between devices with their start and end apart: 21, of which 15 were waited for; matrix products, arithmetic and copies ran while one was open for 12% of the time, Pallas kernels for 0%

profile of v1, /device:TPU:0, one launch (start us, length us, event | category | flops | bytes accessed | tf_op | source)
XLA Modules:
  0.0 220.9 jit_solution(6798835909079258797)
XLA Ops:
  7.2 4.9 %collective-permute-start = (bf16[1,1,256,128]{3,2,1,0:T(8,128)(2,1)}, bf16[1,1,256,128]{3,2,1,0:T(8,128)(2,1)S(1)}, u32[]{:S(2)}, u32[]{:S(2)}) collective-permute-start(bf16[1,1,256,128]{3,2,1,0:T(8,128)(2,1)} %param.3), channel_id=1, source_target_pairs={{0,1},{2,3},{4,5},{6,7},{8,9},{10,11},{12,13},{14,15},{16,17},{18,... | collective-permute-start | bytes 196616 | tf_op jit(solution)/shard_map/ppermute | solution.py:14
  12.1 1.3 collective-permute-start.1
  13.4 0.9 collective-permute-done
  14.3 4.2 %collective-permute-done.1 = bf16[1,1,256,128]{3,2,1,0:T(8,128)(2,1)S(1)} collective-permute-done((bf16[1,1,256,128]{3,2,1,0:T(8,128)(2,1)}, bf16[1,1,256,128]{3,2,1,0:T(8,128)(2,1)S(1)}, u32[]{:S(2)}, u32[]{:S(2)}) %collective-permute-start.1) | collective-permute-done | bytes 65568 | tf_op jit(solution)/shard_map/ppermute | solution.py:15
  18.5 0.9 fusion.23
  19.5 0.9 constant_dynamic-update-slice_fusion.1
  20.5 0.8 copy-done
  21.3 5.2 %convolution_bitcast_fusion = f32[2048,256]{0,1:T(8,128)} fusion(bf16[1152,2048]{1,0:T(8,128)(2,1)} %bitcast.34, bf16[1,1,256,1152]{3,2,1,0:T(8,128)(2,1)S(1)} %slice_dynamic-update-slice_fusion.3), kind=kOutput, calls=%fused_computation.3 | convolution fusion | flops 1207959552 | bytes 7405568 | tf_op jit(solution)/shard_map/dot_general | solution.py:47
  26.6 1.7 collective-permute-start.2
  28.3 1.3 collective-permute-start.3
  29.6 0.6 collective-permute-done.2
  30.2 4.3 %collective-permute-done.3 = bf16[1,1,256,128]{3,2,1,0:T(8,128)(2,1)S(1)} collective-permute-done((bf16[1,1,256,128]{3,2,1,0:T(8,128)(2,1)S(1)}, bf16[1,1,256,128]{3,2,1,0:T(8,128)(2,1)S(1)}, u32[]{:S(2)}, u32[]{:S(2)}) %collective-permute-start.3) | collective-permute-done | bytes 65568 | tf_op jit(solution)/shard_map/ppermute | solution.py:15
  34.5 4.4 %collective-permute-start.5 = (bf16[1,3,256,128]{3,2,1,0:T(8,128)(2,1)S(1)}, bf16[1,3,256,128]{3,2,1,0:T(8,128)(2,1)S(1)}, u32[]{:S(2)}, u32[]{:S(2)}) collective-permute-start(bf16[1,3,256,128]{3,2,1,0:T(8,128)(2,1)S(1)} %constant_dynamic-update-slice_fusion.3), channel_id=1, source_target_pairs={{0,30},{2,0},{4,2},{6,4},{8,6},{10,8},{12,10},{14,12},{16,14},{18,... | collective-permute-start | bytes 589832 | tf_op jit(solution)/shard_map/ppermute | solution.py:65
  39.0 0.4 broadcast_in_dim.3
  39.4 3.1 %collective-permute-done.4 = bf16[1,3,256,128]{3,2,1,0:T(8,128)(2,1)} collective-permute-done((bf16[1,3,256,128]{3,2,1,0:T(8,128)(2,1)S(1)}, bf16[1,3,256,128]{3,2,1,0:T(8,128)(2,1)}, u32[]{:S(2)}, u32[]{:S(2)}) %collective-permute-start.4) | collective-permute-done | bytes 196640 | tf_op jit(solution)/shard_map/ppermute | solution.py:62
  42.5 4.4 %collective-permute-start.7 = (bf16[1,3,256,128]{3,2,1,0:T(8,128)(2,1)S(1)}, bf16[1,3,256,128]{3,2,1,0:T(8,128)(2,1)S(1)}, u32[]{:S(2)}, u32[]{:S(2)}) collective-permute-start(bf16[1,3,256,128]{3,2,1,0:T(8,128)(2,1)S(1)} %collective-permute-done.5), channel_id=1, source_target_pairs={{0,30},{2,0},{4,2},{6,4},{8,6},{10,8},{12,10},{14,12},{16,14},{18,... | collective-permute-start | bytes 589832 | tf_op jit(solution)/shard_map/ppermute | solution.py:65
  47.0 1.0 constant_dynamic-update-slice_fusion.20
  48.0 2.6 %collective-permute-done.6 = bf16[1,3,256,128]{3,2,1,0:T(8,128)(2,1)S(1)} collective-permute-done((bf16[1,3,256,128]{3,2,1,0:T(8,128)(2,1)}, bf16[1,3,256,128]{3,2,1,0:T(8,128)(2,1)S(1)}, u32[]{:S(2)}, u32[]{:S(2)}) %collective-permute-start.6) | collective-permute-done | bytes 196640 | tf_op jit(solution)/shard_map/ppermute | solution.py:62
  50.7 4.4 %collective-permute-start.9 = (bf16[1,3,256,128]{3,2,1,0:T(8,128)(2,1)S(1)}, bf16[1,3,256,128]{3,2,1,0:T(8,128)(2,1)S(1)}, u32[]{:S(2)}, u32[]{:S(2)}) collective-permute-start(bf16[1,3,256,128]{3,2,1,0:T(8,128)(2,1)S(1)} %collective-permute-done.7), channel_id=1, source_target_pairs={{0,30},{2,0},{4,2},{6,4},{8,6},{10,8},{12,10},{14,12},{16,14},{18,... | collective-permute-start | bytes 589832 | tf_op jit(solution)/shard_map/ppermute | solution.py:65
  55.2 3.3 %collective-permute-done.8 = bf16[1,3,256,128]{3,2,1,0:T(8,128)(2,1)S(1)} collective-permute-done((bf16[1,3,256,128]{3,2,1,0:T(8,128)(2,1)S(1)}, bf16[1,3,256,128]{3,2,1,0:T(8,128)(2,1)S(1)}, u32[]{:S(2)}, u32[]{:S(2)}) %collective-permute-start.8) | collective-permute-done | bytes 196640 | tf_op jit(solution)/shard_map/ppermute | solution.py:62
  58.6 1.1 collective-permute-done.9
  59.7 4.7 %collective-permute-start.11 = (bf16[1,3,256,128]{3,2,1,0:T(8,128)(2,1)S(1)}, bf16[1,3,256,128]{3,2,1,0:T(8,128)(2,1)S(1)}, u32[]{:S(2)}, u32[]{:S(2)}) collective-permute-start(bf16[1,3,256,128]{3,2,1,0:T(8,128)(2,1)S(1)} %collective-permute-done.9), channel_id=1, source_target_pairs={{0,30},{2,0},{4,2},{6,4},{8,6},{10,8},{12,10},{14,12},{16,14},{18,... | collective-permute-start | bytes 589832 | tf_op jit(solution)/shard_map/ppermute | solution.py:65
  64.5 2.5 %collective-permute-done.10 = bf16[1,3,256,128]{3,2,1,0:T(8,128)(2,1)S(1)} collective-permute-done((bf16[1,3,256,128]{3,2,1,0:T(8,128)(2,1)S(1)}, bf16[1,3,256,128]{3,2,1,0:T(8,128)(2,1)S(1)}, u32[]{:S(2)}, u32[]{:S(2)}) %collective-permute-start.10) | collective-permute-done | bytes 196640 | tf_op jit(solution)/shard_map/ppermute | solution.py:62
  67.0 1.3 collective-permute-done.11
  68.3 4.7 %collective-permute-start.13 = (bf16[1,3,256,128]{3,2,1,0:T(8,128)(2,1)S(1)}, bf16[1,3,256,128]{3,2,1,0:T(8,128)(2,1)S(1)}, u32[]{:S(2)}, u32[]{:S(2)}) collective-permute-start(bf16[1,3,256,128]{3,2,1,0:T(8,128)(2,1)S(1)} %collective-permute-done.11), channel_id=1, source_target_pairs={{0,30},{2,0},{4,2},{6,4},{8,6},{10,8},{12,10},{14,12},{16,14},{18,... | collective-permute-start | bytes 589832 | tf_op jit(solution)/shard_map/ppermute | solution.py:65
  73.2 3.5 %collective-permute-done.12 = bf16[1,3,256,128]{3,2,1,0:T(8,128)(2,1)S(1)} collective-permute-done((bf16[1,3,256,128]{3,2,1,0:T(8,128)(2,1)S(1)}, bf16[1,3,256,128]{3,2,1,0:T(8,128)(2,1)S(1)}, u32[]{:S(2)}, u32[]{:S(2)}) %collective-permute-start.12) | collective-permute-done | bytes 196640 | tf_op jit(solution)/shard_map/ppermute | solution.py:62
  76.7 4.4 %collective-permute-start.15 = (bf16[1,3,256,128]{3,2,1,0:T(8,128)(2,1)S(1)}, bf16[1,3,256,128]{3,2,1,0:T(8,128)(2,1)S(1)}, u32[]{:S(2)}, u32[]{:S(2)}) collective-permute-start(bf16[1,3,256,128]{3,2,1,0:T(8,128)(2,1)S(1)} %collective-permute-done.13), channel_id=1, source_target_pairs={{0,30},{2,0},{4,2},{6,4},{8,6},{10,8},{12,10},{14,12},{16,14},{18,... | collective-permute-start | bytes 589832 | tf_op jit(solution)/shard_map/ppermute | solution.py:65
  81.3 3.4 %collective-permute-done.14 = bf16[1,3,256,128]{3,2,1,0:T(8,128)(2,1)S(1)} collective-permute-done((bf16[1,3,256,128]{3,2,1,0:T(8,128)(2,1)S(1)}, bf16[1,3,256,128]{3,2,1,0:T(8,128)(2,1)S(1)}, u32[]{:S(2)}, u32[]{:S(2)}) %collective-permute-start.14) | collective-permute-done | bytes 196640 | tf_op jit(solution)/shard_map/ppermute | solution.py:62
  84.6 4.5 %collective-permute-start.17 = (bf16[1,3,256,128]{3,2,1,0:T(8,128)(2,1)S(1)}, bf16[1,3,256,128]{3,2,1,0:T(8,128)(2,1)S(1)}, u32[]{:S(2)}, u32[]{:S(2)}) collective-permute-start(bf16[1,3,256,128]{3,2,1,0:T(8,128)(2,1)S(1)} %collective-permute-done.15), channel_id=1, source_target_pairs={{0,30},{2,0},{4,2},{6,4},{8,6},{10,8},{12,10},{14,12},{16,14},{18,... | collective-permute-start | bytes 589832 | tf_op jit(solution)/shard_map/ppermute | solution.py:65
  89.3 4.8 %collective-permute-done.16 = bf16[1,3,256,128]{3,2,1,0:T(8,128)(2,1)S(1)} collective-permute-done((bf16[1,3,256,128]{3,2,1,0:T(8,128)(2,1)S(1)}, bf16[1,3,256,128]{3,2,1,0:T(8,128)(2,1)S(1)}, u32[]{:S(2)}, u32[]{:S(2)}) %collective-permute-start.16) | collective-permute-done | bytes 196640 | tf_op jit(solution)/shard_map/ppermute | solution.py:62
  94.3 7.6 %collective-permute-done.18 = bf16[1,3,256,128]{3,2,1,0:T(8,128)(2,1)S(1)} collective-permute-done((bf16[1,3,256,128]{3,2,1,0:T(8,128)(2,1)S(1)}, bf16[1,3,256,128]{3,2,1,0:T(8,128)(2,1)S(1)}, u32[]{:S(2)}, u32[]{:S(2)}) %collective-permute-start.18) | collective-permute-done | bytes 196640 | tf_op jit(solution)/shard_map/ppermute | solution.py:62
  102.0 5.1 %convolution_multiply_fusion = f32[1152,2048]{1,0:T(8,128)} fusion(bf16[1,3,256,2048]{3,2,1,0:T(8,128)(2,1)S(1)} %constant_dynamic-update-slice_fusion.6, bf16[1,1,256,1152]{3,2,1,0:T(8,128)(2,1)S(1)} %copy-done.1), kind=kOutput, calls=%fused_computation | convolution fusion | flops 1210318848 | bytes 11075584 | tf_op jit(solution)/shard_map/dot_general | solution.py:79
  107.1 6.8 %copy.6 = bf16[3,3,128,2048]{2,3,1,0:T(8,128)(2,1)} copy(bf16[3,3,128,2048]{3,2,1,0:T(8,128)(2,1)} %param.4) | data formatting | bytes 9437184 | tf_op args[1]
  113.9 4.7 %rev.3 = bf16[3,3,128,2048]{2,3,1,0:T(8,128)(2,1)} reverse(bf16[3,3,128,2048]{2,3,1,0:T(8,128)(2,1)} %copy.6), dimensions={0,1} | reverse | bytes 9437184 | tf_op jit(solution)/shard_map/rev | solution.py:54
  118.6 0.3 fusion.8
  118.9 0.1 slice_dynamic-update-slice_fusion.1
  119.0 0.2 fusion.9
  119.2 0.3 fusion.10
  119.5 0.1 slice_dynamic-update-slice_fusion.2
  119.6 0.2 fusion.11
  119.8 0.3 fusion.12
  120.1 0.1 slice_dynamic-update-slice_fusion
  120.2 0.2 fusion.13
  120.4 1.4 slice-done
  121.8 0.2 slice-done.1
  122.0 3.2 %fusion.5 = bf16[1,1,256,128]{3,2,1,0:T(8,128)(2,1)} fusion(bf16[128,18432]{0,1:T(8,128)(2,1)S(1)} %bitcast.33, bf16[1,1,256,18432]{3,2,1,0:T(8,128)(2,1)S(1)} %fusion.13), kind=kOutput, calls=%fused_computation.11 | convolution fusion | flops 1207992320 | bytes 14221312 | tf_op jit(solution)/shard_map/dot_general | solution.py:75
  125.2 1.6 convert_bitcast_fusion
  126.8 87.3 %reduce-scatter.5.cloned.1.call-done = f32[3,3,128,1024]{3,2,1,0:T(8,128)} async-done(((f32[3,3,128,2048]{3,2,1,0:T(8,128)}), f32[3,3,128,1024]{3,2,1,0:T(8,128)}) %reduce-scatter.5.cloned.1.call-update) | async-done | bytes 4718608 | tf_op jit(solution)/shard_map/reduce_scatter | solution.py:87
  (52 shorter events, 1.4 us)
Async XLA Ops:
  7.2 118.0 %reduce-scatter.3.cloned.1.call-start = ((), (), s32[]{:S(2)}) async-start(), calls=%async_computation.2 | async-start | bytes 2228224 | tf_op jit(solution)/shard_map/reduce_scatter | solution.py:46
  7.2 7.1 %collective-permute-start = (bf16[1,1,256,128]{3,2,1,0:T(8,128)(2,1)}, bf16[1,1,256,128]{3,2,1,0:T(8,128)(2,1)S(1)}, u32[]{:S(2)}, u32[]{:S(2)}) collective-permute-start(bf16[1,1,256,128]{3,2,1,0:T(8,128)(2,1)} %param.3), channel_id=1, source_target_pairs={{0,1},{2,3},{4,5},{6,7},{8,9},{10,11},{12,13},{14,15},{16,17},{18,... | collective-permute-start | bytes 196616 | tf_op jit(solution)/shard_map/ppermute | solution.py:14
  12.1 6.4 %collective-permute-start.1 = (bf16[1,1,256,128]{3,2,1,0:T(8,128)(2,1)}, bf16[1,1,256,128]{3,2,1,0:T(8,128)(2,1)S(1)}, u32[]{:S(2)}, u32[]{:S(2)}) collective-permute-start(bf16[1,1,256,128]{3,2,1,0:T(8,128)(2,1)} %param.3), channel_id=1, source_target_pairs={{1,0},{3,2},{5,4},{7,6},{9,8},{11,10},{13,12},{15,14},{17,16},{19,... | collective-permute-start | bytes 196616 | tf_op jit(solution)/shard_map/ppermute | solution.py:15
  20.5 0.8 copy-start
  21.3 5.3 %copy-start.2 = (bf16[1,1,256,128]{3,2,1,0:T(8,128)(2,1)S(1)}, bf16[1,1,256,128]{3,2,1,0:T(8,128)(2,1)}, u32[]{:S(2)}) copy-start(bf16[1,1,256,128]{3,2,1,0:T(8,128)(2,1)} %param.5) | copy-start | bytes 196612
  26.6 187.5 %reduce-scatter.5.cloned.1.call-start = ((), (), s32[]{:S(2)}) async-start(), calls=%async_computation.3 | async-start | bytes 14155776 | tf_op jit(solution)/shard_map/reduce_scatter | solution.py:87
  26.6 3.6 %collective-permute-start.2 = (bf16[1,1,256,128]{3,2,1,0:T(8,128)(2,1)S(1)}, bf16[1,1,256,128]{3,2,1,0:T(8,128)(2,1)S(1)}, u32[]{:S(2)}, u32[]{:S(2)}) collective-permute-start(bf16[1,1,256,128]{3,2,1,0:T(8,128)(2,1)S(1)} %copy-done.2), channel_id=1, source_target_pairs={{0,1},{2,3},{4,5},{6,7},{8,9},{10,11},{12,13},{14,15},{16,17},{18,... | collective-permute-start | bytes 196616 | tf_op jit(solution)/shard_map/ppermute | solution.py:14
  28.3 6.2 %collective-permute-start.3 = (bf16[1,1,256,128]{3,2,1,0:T(8,128)(2,1)S(1)}, bf16[1,1,256,128]{3,2,1,0:T(8,128)(2,1)S(1)}, u32[]{:S(2)}, u32[]{:S(2)}) collective-permute-start(bf16[1,1,256,128]{3,2,1,0:T(8,128)(2,1)S(1)} %copy-done.2), channel_id=1, source_target_pairs={{1,0},{3,2},{5,4},{7,6},{9,8},{11,10},{13,12},{15,14},{17,16},{19,... | collective-permute-start | bytes 196616 | tf_op jit(solution)/shard_map/ppermute | solution.py:15
  34.5 8.1 %collective-permute-start.4 = (bf16[1,3,256,128]{3,2,1,0:T(8,128)(2,1)S(1)}, bf16[1,3,256,128]{3,2,1,0:T(8,128)(2,1)}, u32[]{:S(2)}, u32[]{:S(2)}) collective-permute-start(bf16[1,3,256,128]{3,2,1,0:T(8,128)(2,1)S(1)} %constant_dynamic-update-slice_fusion.3), channel_id=1, source_target_pairs={{0,2},{2,4},{4,6},{6,8},{8,10},{10,12},{12,14},{14,16},{16,18},{18... | collective-permute-start | bytes 589832 | tf_op jit(solution)/shard_map/ppermute | solution.py:62
  34.5 8.0 %collective-permute-start.5 = (bf16[1,3,256,128]{3,2,1,0:T(8,128)(2,1)S(1)}, bf16[1,3,256,128]{3,2,1,0:T(8,128)(2,1)S(1)}, u32[]{:S(2)}, u32[]{:S(2)}) collective-permute-start(bf16[1,3,256,128]{3,2,1,0:T(8,128)(2,1)S(1)} %constant_dynamic-update-slice_fusion.3), channel_id=1, source_target_pairs={{0,30},{2,0},{4,2},{6,4},{8,6},{10,8},{12,10},{14,12},{16,14},{18,... | collective-permute-start | bytes 589832 | tf_op jit(solution)/shard_map/ppermute | solution.py:65
  39.4 62.6 %copy-start.1 = (bf16[1,1,256,1152]{3,2,1,0:T(8,128)(2,1)S(1)}, bf16[1,1,256,1152]{3,2,1,0:T(8,128)(2,1)}, u32[]{:S(2)}) copy-start(bf16[1,1,256,1152]{3,2,1,0:T(8,128)(2,1)} %copy-done) | copy-start | bytes 1769476
  42.5 8.1 %collective-permute-start.6 = (bf16[1,3,256,128]{3,2,1,0:T(8,128)(2,1)}, bf16[1,3,256,128]{3,2,1,0:T(8,128)(2,1)S(1)}, u32[]{:S(2)}, u32[]{:S(2)}) collective-permute-start(bf16[1,3,256,128]{3,2,1,0:T(8,128)(2,1)} %collective-permute-done.4), channel_id=1, source_target_pairs={{0,2},{2,4},{4,6},{6,8},{8,10},{10,12},{12,14},{14,16},{16,18},{18... | collective-permute-start | bytes 589832 | tf_op jit(solution)/shard_map/ppermute | solution.py:62
  42.5 8.1 %collective-permute-start.7 = (bf16[1,3,256,128]{3,2,1,0:T(8,128)(2,1)S(1)}, bf16[1,3,256,128]{3,2,1,0:T(8,128)(2,1)S(1)}, u32[]{:S(2)}, u32[]{:S(2)}) collective-permute-start(bf16[1,3,256,128]{3,2,1,0:T(8,128)(2,1)S(1)} %collective-permute-done.5), channel_id=1, source_target_pairs={{0,30},{2,0},{4,2},{6,4},{8,6},{10,8},{12,10},{14,12},{16,14},{18,... | collective-permute-start | bytes 589832 | tf_op jit(solution)/shard_map/ppermute | solution.py:65
  50.6 7.9 %collective-permute-start.8 = (bf16[1,3,256,128]{3,2,1,0:T(8,128)(2,1)S(1)}, bf16[1,3,256,128]{3,2,1,0:T(8,128)(2,1)S(1)}, u32[]{:S(2)}, u32[]{:S(2)}) collective-permute-start(bf16[1,3,256,128]{3,2,1,0:T(8,128)(2,1)S(1)} %collective-permute-done.6), channel_id=1, source_target_pairs={{0,2},{2,4},{4,6},{6,8},{8,10},{10,12},{12,14},{14,16},{16,18},{18... | collective-permute-start | bytes 589832 | tf_op jit(solution)/shard_map/ppermute | solution.py:62
  50.7 9.0 %collective-permute-start.9 = (bf16[1,3,256,128]{3,2,1,0:T(8,128)(2,1)S(1)}, bf16[1,3,256,128]{3,2,1,0:T(8,128)(2,1)S(1)}, u32[]{:S(2)}, u32[]{:S(2)}) collective-permute-start(bf16[1,3,256,128]{3,2,1,0:T(8,128)(2,1)S(1)} %collective-permute-done.7), channel_id=1, source_target_pairs={{0,30},{2,0},{4,2},{6,4},{8,6},{10,8},{12,10},{14,12},{16,14},{18,... | collective-permute-start | bytes 589832 | tf_op jit(solution)/shard_map/ppermute | solution.py:65
  58.6 8.5 %collective-permute-start.10 = (bf16[1,3,256,128]{3,2,1,0:T(8,128)(2,1)S(1)}, bf16[1,3,256,128]{3,2,1,0:T(8,128)(2,1)S(1)}, u32[]{:S(2)}, u32[]{:S(2)}) collective-permute-start(bf16[1,3,256,128]{3,2,1,0:T(8,128)(2,1)S(1)} %collective-permute-done.8), channel_id=1, source_target_pairs={{0,2},{2,4},{4,6},{6,8},{8,10},{10,12},{12,14},{14,16},{16,18},{18... | collective-permute-start | bytes 589832 | tf_op jit(solution)/shard_map/ppermute | solution.py:62
  59.7 8.6 %collective-permute-start.11 = (bf16[1,3,256,128]{3,2,1,0:T(8,128)(2,1)S(1)}, bf16[1,3,256,128]{3,2,1,0:T(8,128)(2,1)S(1)}, u32[]{:S(2)}, u32[]{:S(2)}) collective-permute-start(bf16[1,3,256,128]{3,2,1,0:T(8,128)(2,1)S(1)} %collective-permute-done.9), channel_id=1, source_target_pairs={{0,30},{2,0},{4,2},{6,4},{8,6},{10,8},{12,10},{14,12},{16,14},{18,... | collective-permute-start | bytes 589832 | tf_op jit(solution)/shard_map/ppermute | solution.py:65
  67.0 9.7 %collective-permute-start.12 = (bf16[1,3,256,128]{3,2,1,0:T(8,128)(2,1)S(1)}, bf16[1,3,256,128]{3,2,1,0:T(8,128)(2,1)S(1)}, u32[]{:S(2)}, u32[]{:S(2)}) collective-permute-start(bf16[1,3,256,128]{3,2,1,0:T(8,128)(2,1)S(1)} %collective-permute-done.10), channel_id=1, source_target_pairs={{0,2},{2,4},{4,6},{6,8},{8,10},{10,12},{12,14},{14,16},{16,18},{18... | collective-permute-start | bytes 589832 | tf_op jit(solution)/shard_map/ppermute | solution.py:62
  68.3 8.4 %collective-permute-start.13 = (bf16[1,3,256,128]{3,2,1,0:T(8,128)(2,1)S(1)}, bf16[1,3,256,128]{3,2,1,0:T(8,128)(2,1)S(1)}, u32[]{:S(2)}, u32[]{:S(2)}) collective-permute-start(bf16[1,3,256,128]{3,2,1,0:T(8,128)(2,1)S(1)} %collective-permute-done.11), channel_id=1, source_target_pairs={{0,30},{2,0},{4,2},{6,4},{8,6},{10,8},{12,10},{14,12},{16,14},{18,... | collective-permute-start | bytes 589832 | tf_op jit(solution)/shard_map/ppermute | solution.py:65
  76.7 7.9 %collective-permute-start.14 = (bf16[1,3,256,128]{3,2,1,0:T(8,128)(2,1)S(1)}, bf16[1,3,256,128]{3,2,1,0:T(8,128)(2,1)S(1)}, u32[]{:S(2)}, u32[]{:S(2)}) collective-permute-start(bf16[1,3,256,128]{3,2,1,0:T(8,128)(2,1)S(1)} %collective-permute-done.12), channel_id=1, source_target_pairs={{0,2},{2,4},{4,6},{6,8},{8,10},{10,12},{12,14},{14,16},{16,18},{18... | collective-permute-start | bytes 589832 | tf_op jit(solution)/shard_map/ppermute | solution.py:62
  76.7 7.9 %collective-permute-start.15 = (bf16[1,3,256,128]{3,2,1,0:T(8,128)(2,1)S(1)}, bf16[1,3,256,128]{3,2,1,0:T(8,128)(2,1)S(1)}, u32[]{:S(2)}, u32[]{:S(2)}) collective-permute-start(bf16[1,3,256,128]{3,2,1,0:T(8,128)(2,1)S(1)} %collective-permute-done.13), channel_id=1, source_target_pairs={{0,30},{2,0},{4,2},{6,4},{8,6},{10,8},{12,10},{14,12},{16,14},{18,... | collective-permute-start | bytes 589832 | tf_op jit(solution)/shard_map/ppermute | solution.py:65
  84.6 9.5 %collective-permute-start.16 = (bf16[1,3,256,128]{3,2,1,0:T(8,128)(2,1)S(1)}, bf16[1,3,256,128]{3,2,1,0:T(8,128)(2,1)S(1)}, u32[]{:S(2)}, u32[]{:S(2)}) collective-permute-start(bf16[1,3,256,128]{3,2,1,0:T(8,128)(2,1)S(1)} %collective-permute-done.14), channel_id=1, source_target_pairs={{0,2},{2,4},{4,6},{6,8},{8,10},{10,12},{12,14},{14,16},{16,18},{18... | collective-permute-start | bytes 589832 | tf_op jit(solution)/shard_map/ppermute | solution.py:62
  84.6 9.6 %collective-permute-start.17 = (bf16[1,3,256,128]{3,2,1,0:T(8,128)(2,1)S(1)}, bf16[1,3,256,128]{3,2,1,0:T(8,128)(2,1)S(1)}, u32[]{:S(2)}, u32[]{:S(2)}) collective-permute-start(bf16[1,3,256,128]{3,2,1,0:T(8,128)(2,1)S(1)} %collective-permute-done.15), channel_id=1, source_target_pairs={{0,30},{2,0},{4,2},{6,4},{8,6},{10,8},{12,10},{14,12},{16,14},{18,... | collective-permute-start | bytes 589832 | tf_op jit(solution)/shard_map/ppermute | solution.py:65
  94.1 7.8 %collective-permute-start.18 = (bf16[1,3,256,128]{3,2,1,0:T(8,128)(2,1)S(1)}, bf16[1,3,256,128]{3,2,1,0:T(8,128)(2,1)S(1)}, u32[]{:S(2)}, u32[]{:S(2)}) collective-permute-start(bf16[1,3,256,128]{3,2,1,0:T(8,128)(2,1)S(1)} %collective-permute-done.16), channel_id=1, source_target_pairs={{0,2},{2,4},{4,6},{6,8},{8,10},{10,12},{12,14},{14,16},{16,18},{18... | collective-permute-start | bytes 589832 | tf_op jit(solution)/shard_map/ppermute | solution.py:62
  119.6 2.2 %slice-start = ((s8[4718592]{0:T(1024)(128)(4,1)}), s8[4194304]{0:T(1024)(128)(4,1)S(1)}, s32[]{:S(2)}) async-start(s8[4718592]{0:T(1024)(128)(4,1)} %bitcast.31), calls=%async_computation.4 | async-start | bytes 8388608
  119.8 2.1 slice-start.1
Sparse Core Ops, SparseCore 0:
  26.7 67.6 reduce-scatter.2
  107.2 106.7 reduce-scatter.4
